TPU v7x, 256 devices: a whole 4x4x8 slice. The times are simulated.
256 devices in a mesh: dp: 32 (over x, z), mp: 8 (over y, core).
Axes of the slice: x: 4, y: 4, z: 8, core: 2. Of those that a mesh axis runs over, the one named last changes fastest.
Arguments:
- vision: bfloat16 [8192, 3200], P(('dp', 'mp')), may hold values from -6 to 6
- vision_gain: float32 [3200], replicated, may hold values from 0.1 to 1.9
- image_slot: int32 [32], replicated, may hold values from 0 to 63, as said below
- text_embed: bfloat16 [16384, 8192], P('dp', 'mp'), may hold values from -6 to 6
- w_proj: bfloat16 [3200, 8192], P(None, 'mp'), may hold values from -0.109375 to 0.109375
- llm_gain: float32 [8192], P('mp'), may hold values from 0.1 to 1.9
- w_key: bfloat16 [8192, 1024], P('mp'), may hold values from -0.0625 to 0.0625
- w_value: bfloat16 [8192, 1024], P('mp'), may hold values from -0.0625 to 0.0625
- key_grad: bfloat16 [16384, 1024], P('dp', 'mp'), may hold values from -6 to 6
- value_grad: bfloat16 [16384, 1024], P('dp', 'mp'), may hold values from -6 to 6
Outputs:
- key_out: bfloat16 [16384, 1024], P('dp', 'mp')
- value_out: bfloat16 [16384, 1024], P('dp', 'mp')
- text_grad: bfloat16 [16384, 8192], P('dp', 'mp')
- vision_grad: bfloat16 [8192, 3200], P(('dp', 'mp'))
Inputs may be any that keep to these rules, and one draw needn't show every extreme that they name: `image_slot`: the 32 entries are different slots. Image i is encoded on index i of dp; slot j covers positions j * 256 to (j + 1) * 256 - 1, so it lies on index j // 2 of dp. One index of dp receives 2 images, every other one at most one.
All inputs are finite; a program needn't handle non-finite values.
Results may differ from a plain program's by a relative error of at most 0.0058.
Values may be sent and summed in bfloat16 or wider, within the bound.
No kernel may reach another device: no remote copies, remote signals or barrier semaphores. Data moves between devices by JAX's collectives and lax.ppermute only.
A program may use at most 128 MiB of HBM per device.

v0:
```python
import jax
import jax.numpy as jnp
from jax import lax
from jax.sharding import PartitionSpec as P

D = 8192
PATCH = 256


def side_by_side(arrays, axis, dim, along):
    both = jnp.concatenate(arrays, axis=along)
    result, at, finished = (lax.psum_scatter(both, axis, scatter_dimension=dim, tiled=True), 0, [])
    for a in arrays:
        finished.append(lax.slice_in_dim(result, at, at + a.shape[along], axis=along))
        at += a.shape[along]
    return tuple(finished)


def shards(
    vision,
    vision_gain,
    image_slot,
    text_embed,
    w_proj,
    llm_gain,
    w_key,
    w_value,
    key_grad,
    value_grad,
):
    dp_count = lax.axis_size("dp")
    here = lax.axis_index("dp")
    slot_dev = text_embed.shape[0] // PATCH
    img_rows = vision.shape[0]
    width_dev = text_embed.shape[1]
    vision_f = vision.astype(jnp.float32)
    vis_scale = lax.rsqrt(jnp.mean(vision_f * vision_f, axis=1, keepdims=True) + 1e-06)
    vis_normed = (vision_f * vis_scale * vision_gain).astype(jnp.bfloat16)
    dest_all = image_slot // slot_dev
    within_all = image_slot % slot_dev
    mine = dest_all == here
    pick_mask = (within_all[None, :] == jnp.arange(slot_dev, dtype=jnp.int32)[:, None]) & mine[
        None, :
    ]
    filled = jnp.sum(pick_mask.astype(jnp.float32), axis=1) > 0.5
    slot_ids = jnp.arange(dp_count * slot_dev, dtype=jnp.int32)
    slot_pick = (slot_ids[:, None] == image_slot[None, :]).astype(jnp.bfloat16)
    spread = lax.all_to_all(vis_normed[None], "dp", split_axis=2, concat_axis=0, tiled=True)
    packed = jnp.einsum(
        "ji,irc->jrc", slot_pick, spread, preferred_element_type=jnp.float32
    ).astype(jnp.bfloat16)
    packed = packed.reshape(dp_count, slot_dev, img_rows, spread.shape[2])
    arrived = lax.all_to_all(packed, "dp", split_axis=0, concat_axis=3, tiled=True)[0]
    image_embed = jnp.einsum(
        "srv,vd->srd",
        lax.all_gather(arrived, "mp", axis=1, tiled=True),
        w_proj,
        preferred_element_type=jnp.float32,
    ).astype(jnp.bfloat16)
    text_blocks = text_embed.reshape(slot_dev, PATCH, width_dev)
    embed = jnp.where(filled[:, None, None], image_embed, text_blocks).reshape(
        slot_dev * PATCH, width_dev
    )
    embed_f = embed.astype(jnp.float32)
    square_total = lax.psum(jnp.sum(embed_f * embed_f, axis=1), "mp")
    scale = lax.rsqrt(square_total / D + 1e-05)[:, None]
    llm_normed = (embed_f * scale * llm_gain).astype(jnp.bfloat16)
    key_part = jnp.dot(llm_normed, w_key, preferred_element_type=jnp.float32)
    value_part = jnp.dot(llm_normed, w_value, preferred_element_type=jnp.float32)
    key_sum, value_sum = side_by_side((key_part, value_part), "mp", 1, 0)
    key_out = key_sum.astype(jnp.bfloat16)
    value_out = value_sum.astype(jnp.bfloat16)
    stacked = jnp.stack([key_grad, value_grad])
    piece = lax.all_gather(stacked, "mp", axis=2, tiled=True)
    contract = (((1,), (1,)), ((), ()))
    carry = lax.dot_general(piece[0], w_key, contract, preferred_element_type=jnp.float32)
    d_normed = carry + lax.dot_general(
        piece[1], w_value, contract, preferred_element_type=jnp.float32
    )
    grad_g = d_normed * llm_gain
    inner_total = lax.psum(jnp.sum(grad_g * embed_f, axis=1), "mp")
    d_embed = scale * grad_g - embed_f * scale * scale * scale * (inner_total / D)[:, None]
    d_blocks = d_embed.reshape(slot_dev, PATCH, width_dev)
    text_grad = (
        jnp.where(filled[:, None, None], 0.0, d_blocks)
        .reshape(slot_dev * PATCH, width_dev)
        .astype(jnp.bfloat16)
    )
    image_grad = d_blocks.astype(jnp.bfloat16)
    piece = image_grad
    d_vis_rows = lax.psum_scatter(
        jnp.einsum("srd,vd->rsv", piece, w_proj, preferred_element_type=jnp.float32),
        "mp",
        scatter_dimension=0,
        tiled=True,
    )
    d_vis_slots = jnp.transpose(d_vis_rows, (1, 0, 2)).astype(jnp.bfloat16)
    spread_back = lax.all_to_all(d_vis_slots[None], "dp", split_axis=3, concat_axis=0, tiled=True)
    spread_back = spread_back.reshape(dp_count * slot_dev, img_rows, spread_back.shape[3])
    per_image = jnp.einsum(
        "ji,jrc->irc", slot_pick, spread_back, preferred_element_type=jnp.float32
    ).astype(jnp.bfloat16)
    d_vis = lax.all_to_all(per_image, "dp", split_axis=0, concat_axis=2, tiled=True)[0].astype(
        jnp.float32
    )
    grad_h = d_vis * vision_gain
    vis_inner = jnp.mean(grad_h * vision_f, axis=1, keepdims=True)
    vision_grad = vis_scale * grad_h - vision_f * vis_scale * vis_scale * vis_scale * vis_inner
    return (key_out, value_out, text_grad, vision_grad.astype(jnp.bfloat16))


def solution(mesh):
    placed = (
        P(("dp", "mp"), None),
        P(),
        P(),
        P("dp", "mp"),
        P(None, "mp"),
        P("mp"),
        P("mp", None),
        P("mp", None),
        P("dp", "mp"),
        P("dp", "mp"),
    )
    return jax.shard_map(
        shards,
        mesh=mesh,
        in_specs=placed,
        out_specs=(P("dp", "mp"), P("dp", "mp"), P("dp", "mp"), P(("dp", "mp"), None)),
        check_vma=False,
    )
```

profile of v0, /device:TPU:2, one launch (start us, length us, event | category | flops | bytes accessed | tf_op | source)
XLA Modules:
  0.0 260.3 jit_solution(9408439830672868749)
XLA Ops:
  7.2 1.9 pad_maximum_fusion.1
  11.3 2.9 %copy.33 = bf16[1,32,3200]{1,0,2:T(2,128)(2,1)} copy(bf16[1,32,3200]{2,1,0:T(8,128)(2,1)S(1)} %fusion.32) | data formatting | bytes 409600 | tf_op jit(solution)/shard_map/broadcast_in_dim | solution.py:48
  14.7 18.6 %reduce.1 = bf16[3200,32]{1,0:T(8,128)(2,1)S(1)} reduce(bf16[3200,1,32]{2,1,0:T(2,128)(2,1)} %bitcast.95, bf16[]{:T(256)} %broadcast.74), dimensions={1}, to_apply=%bitcast.78.reduce_sub_computation | reduce | bytes 409602
  34.0 21.8 %all_to_all.57 = bf16[32,2,1600]{2,1,0:T(2,128)(2,1)S(1)} all-to-all(bf16[32,2,1600]{2,1,0:T(2,128)(2,1)S(1)} %reshape.62), channel_id=1, replica_groups=mesh['dp'=32,'mp'=8] {'dp'}, dimensions={0} | all-to-all | bytes 409600 | tf_op jit(solution)/shard_map/all_to_all | solution.py:48
  55.8 2.1 reshape.63
  57.9 3.4 %copy.34 = bf16[1,32,3200]{2,1,0:T(8,128)(2,1)S(1)} copy(bf16[1,32,3200]{1,0,2:T(2,128)(2,1)} %bitcast.96) | data formatting | bytes 409600 | tf_op jit(solution)/shard_map/all_to_all | solution.py:48
  63.2 20.0 %all_to_all.58 = bf16[32,2,32,100]{3,1,2,0:T(2,128)(2,1)S(1)} all-to-all(bf16[32,2,32,100]{3,1,2,0:T(2,128)(2,1)S(1)} %copy.35), channel_id=1, replica_groups=mesh['dp'=32,'mp'=8] {'dp'}, dimensions={0} | all-to-all | bytes 819200 | tf_op jit(solution)/shard_map/all_to_all | solution.py:53
  85.6 4.6 %fusion.21 = f32[512,1024]{1,0:T(8,128)} fusion(bf16[1024,1024]{1,0:T(8,128)(2,1)} %param.16, bf16[2,512,1024]{2,1,0:T(8,128)(2,1)} %all-gather.5.cloned.1.call-done), kind=kOutput, calls=%fused_computation.25 | convolution fusion | flops 1073741824 | bytes 5242880 | tf_op jit(solution)/shard_map/dot_general | solution.py:76
  90.1 24.3 %all-gather.3.cloned.1.call-done = bf16[2,256,3200]{2,1,0:T(8,128)(2,1)} async-done(((bf16[2,32,3200]{2,1,0:T(8,128)(2,1)}), bf16[2,256,3200]{2,1,0:T(8,128)(2,1)}) %all-gather.3.cloned.1.call-update) | async-done | bytes 3276816 | tf_op jit(solution)/shard_map/all_gather | solution.py:56
  114.4 8.0 %fusion.13 = (f32[2,256]{1,0:T(2,128)S(1)}, bf16[2,256,1024]{2,1,0:T(8,128)(2,1)S(1)}) fusion(bf16[2,256,1024]{2,1,0:T(8,128)(2,1)} %bitcast.107, bf16[2,256,3200]{2,1,0:T(8,128)(2,1)} %all-gather.3.cloned.1.call-done, bf16[3200,1024]{1,0:T(8,128)(2,1)} %param.14, pred[2]{0:T(512)(128)(4,1)S(1)} %broadcast_compare_fusion), kind=kOutput, calls=%fused_computation.15 | convolution fusion | flops 3358064128 | bytes 11929602 | tf_op jit(solution)/shard_map/srv,vd->srd/dot_general | solution.py:54
  122.5 2.7 %fusion.14 = (f32[512]{0:T(512)S(1)}, f32[512,1024]{1,0:T(8,128)}) fusion(bf16[2,256,1024]{2,1,0:T(8,128)(2,1)S(1)} %get-tuple-element.16, f32[1024]{0:T(1024)S(1)} %copy-done.6, f32[512,1024]{1,0:T(8,128)S(1)} %copy-done.2, bf16[1024,1024]{1,0:T(8,128)(2,1)S(1)} %copy-done, bf16[2,512,1024]{2,1,0:T(8,128)(2,1)S(1)} %copy-done.4), kind=kOutput, calls=%fused_computation.16 | convolution fusion | flops 1076362752 | bytes 8394752 | tf_op jit(solution)/shard_map/dot_general | solution.py:77
  125.2 13.7 %all-reduce = (f32[512]{0:T(512)S(1)}, f32[512]{0:T(512)S(1)}) all-reduce(f32[512]{0:T(512)S(1)} %bitcast.105, f32[512]{0:T(512)S(1)} %get-tuple-element.17), channel_id=1, replica_groups=mesh['dp'=32,'mp'=8] {'mp'}, use_global_device_ids=true, to_apply=%region_3.4 | all-reduce | flops 1024 | bytes 8192 | tf_op jit(solution)/shard_map/psum | solution.py:65
  138.8 3.6 %fusion.40 = (bf16[512,1024]{1,0:T(8,128)(2,1)S(1)}, bf16[512,1024]{1,0:T(8,128)(2,1)}, bf16[512,1024]{1,0:T(8,128)(2,1)}) fusion(f32[512]{0:T(512)S(1)} %get-tuple-element.20, bf16[2,256,1024]{2,1,0:T(8,128)(2,1)S(1)} %get-tuple-element.16, f32[512,1024]{1,0:T(8,128)} %get-tuple-element.18, f32[512]{0:T(512)S(1)} %get-tuple-element.19, ...), kind=kLoop, calls=%fused_computation.60 | loop fusion | flops 6291456 | bytes 6300160 | tf_op jit(solution)/shard_map/convert_element_type | solution.py:89
  142.5 8.6 %fusion.4 = f32[256,2,3200]{2,0,1:T(8,128)} fusion(bf16[2,256,1024]{2,1,0:T(8,128)(2,1)S(1)} %bitcast.102, bf16[3200,1024]{1,0:T(8,128)(2,1)} %param.14), kind=kOutput, calls=%fused_computation.4 | convolution fusion | flops 3355443200 | bytes 14155776 | tf_op jit(solution)/shard_map/srd,vd->rsv/dot_general | solution.py:92
  152.3 2.8 %fusion.42 = f32[512,1024]{1,0:T(8,128)S(1)} fusion(bf16[512,1024]{1,0:T(8,128)(2,1)S(1)} %copy-done.3, bf16[1024,1024]{1,0:T(8,128)(2,1)} %param.16), kind=kOutput, calls=%fused_computation.62 | convolution fusion | flops 1073741824 | bytes 5242880 | tf_op jit(solution)/shard_map/dot_general | solution.py:68
  156.4 2.6 pad_maximum_fusion
  159.0 37.4 %reduce-scatter.5.cloned.1.call-done = f32[32,2,3200]{2,0,1:T(8,128)} async-done(((f32[256,2,3200]{2,0,1:T(8,128)}), f32[32,2,3200]{2,0,1:T(8,128)}) %reduce-scatter.5.cloned.1.call-update) | async-done | bytes 819216 | tf_op jit(solution)/shard_map/reduce_scatter | solution.py:91
  197.5 2.9 %copy.37 = bf16[1,2,32,3200]{2,1,0,3:T(2,128)(2,1)} copy(bf16[1,2,32,3200]{3,2,1,0:T(8,128)(2,1)S(1)} %convert_bitcast_fusion.1) | data formatting | bytes 819200 | tf_op jit(solution)/shard_map/broadcast_in_dim | solution.py:98
  200.4 4.3 %reshape.64 = bf16[32,2,3200]{2,1,0:T(2,128)(2,1)S(1)} reshape(bf16[3200,1,2,32]{3,2,1,0:T(2,128)(2,1)} %bitcast.97) | data formatting | bytes 819200
  204.7 22.9 %all_to_all.59 = bf16[32,2,3200]{2,1,0:T(2,128)(2,1)S(1)} all-to-all(bf16[32,2,3200]{2,1,0:T(2,128)(2,1)S(1)} %reshape.64), channel_id=1, replica_groups=mesh['dp'=32,'mp'=8] {'dp'}, dimensions={0} | all-to-all | bytes 819200 | tf_op jit(solution)/shard_map/all_to_all | solution.py:98
  227.6 2.1 reshape.65
  229.7 4.6 %copy.38 = bf16[1,2,32,32,100]{4,1,3,2,0:T(2,128)(2,1)S(1)} copy(bf16[1,2,32,32,100]{2,1,4,3,0:T(2,128)(2,1)} %bitcast.98) | data formatting | bytes 819200 | tf_op jit(solution)/shard_map/all_to_all | solution.py:98
  235.4 6.5 %all-to-all-start.3 = ((bf16[32,32,100]{2,1,0:T(8,128)(2,1)}), bf16[32,32,100]{2,1,0:T(8,128)(2,1)S(1)}, u32[]{:S(2)}, u32[]{:S(2)}) async-start(bf16[32,32,100]{2,1,0:T(8,128)(2,1)} %copy.39), calls=%async_computation.5 | async-start | bytes 524288 | tf_op jit(solution)/shard_map/all_to_all | solution.py:103
  243.8 8.2 %all-to-all-done.3 = bf16[32,32,100]{2,1,0:T(8,128)(2,1)S(1)} async-done(((bf16[32,32,100]{2,1,0:T(8,128)(2,1)}), bf16[32,32,100]{2,1,0:T(8,128)(2,1)S(1)}, u32[]{:S(2)}, u32[]{:S(2)}) %all-to-all-start.3) | async-done | bytes 204832 | tf_op jit(solution)/shard_map/all_to_all | solution.py:103
  (56 shorter events, 16.1 us)
Async XLA Ops:
  7.2 115.3 %copy-start = (bf16[1024,1024]{1,0:T(8,128)(2,1)S(1)}, bf16[1024,1024]{1,0:T(8,128)(2,1)}, u32[]{:S(2)}) copy-start(bf16[1024,1024]{1,0:T(8,128)(2,1)} %param.17) | copy-start | bytes 6291460
  7.2 78.4 %all-gather.5.cloned.1.call-start = ((), (), s32[]{:S(2)}) async-start(), calls=%async_computation.8 | async-start | bytes 2359296 | tf_op jit(solution)/shard_map/all_gather | solution.py:74
  9.1 105.3 %all-gather.3.cloned.1.call-start = ((), (), s32[]{:S(2)}) async-start(), calls=%async_computation.6 | async-start | bytes 3686400 | tf_op jit(solution)/shard_map/all_gather | solution.py:56
  55.8 6.5 %copy-start.7 = (s32[32]{0:T(128)S(1)}, s32[32]{0:T(128)}, u32[]{:S(2)}) copy-start(s32[32]{0:T(128)} %param.12) | copy-start | bytes 388
  85.1 111.3 %reduce-scatter.5.cloned.1.call-start = ((), (), s32[]{:S(2)}) async-start(), calls=%async_computation.9 | async-start | bytes 7372800 | tf_op jit(solution)/shard_map/reduce_scatter | solution.py:91
  114.4 8.0 %copy-start.2 = (f32[512,1024]{1,0:T(8,128)S(1)}, f32[512,1024]{1,0:T(8,128)}, u32[]{:S(2)}) copy-start(f32[512,1024]{1,0:T(8,128)} %fusion.21) | copy-start | bytes 6291460
  114.4 8.0 %copy-start.4 = (bf16[2,512,1024]{2,1,0:T(8,128)(2,1)S(1)}, bf16[2,512,1024]{2,1,0:T(8,128)(2,1)}, u32[]{:S(2)}) copy-start(bf16[2,512,1024]{2,1,0:T(8,128)(2,1)} %all-gather.5.cloned.1.call-done) | copy-start | bytes 6291460
  114.4 8.0 %copy-start.6 = (f32[1024]{0:T(1024)S(1)}, f32[1024]{0:T(1024)}, u32[]{:S(2)}) copy-start(f32[1024]{0:T(1024)} %param.15) | copy-start | bytes 12292
  151.0 1.2 copy-start.3
  151.1 90.9 %reduce-scatter.3.cloned.1.call-start = ((), (), s32[]{:S(2)}) async-start(), calls=%async_computation.7 | async-start | bytes 4718592 | tf_op jit(solution)/shard_map/reduce_scatter | solution.py:12
  235.4 16.6 %all-to-all-start.3 = ((bf16[32,32,100]{2,1,0:T(8,128)(2,1)}), bf16[32,32,100]{2,1,0:T(8,128)(2,1)S(1)}, u32[]{:S(2)}, u32[]{:S(2)}) async-start(bf16[32,32,100]{2,1,0:T(8,128)(2,1)} %copy.39), calls=%async_computation.5 | async-start | bytes 524288 | tf_op jit(solution)/shard_map/all_to_all | solution.py:103
  241.9 10.8 %copy-start.1 = (bf16[32,3200]{1,0:T(8,128)(2,1)S(1)}, bf16[32,3200]{1,0:T(8,128)(2,1)}, u32[]{:S(2)}) copy-start(bf16[32,3200]{1,0:T(8,128)(2,1)} %param.10) | copy-start | bytes 614404
  241.9 10.8 %copy-start.5 = (f32[3200]{0:T(1024)S(1)}, f32[3200]{0:T(1024)}, u32[]{:S(2)}) copy-start(f32[3200]{0:T(1024)} %param.11) | copy-start | bytes 38404
Sparse Core Ops, SparseCore 0:
  9.8 32.7 all-gather.4
  85.2 29.1 all-gather.2
  151.2 45.1 reduce-scatter.4
  198.8 40.6 reduce-scatter.2
where the time goes:
time: 263 us; the launch traced here: 260 us
  blocking collectives  78.3 us (30%)
  waiting for transfers between devices  70 us (27%)
  other arithmetic  32.4 us (12%)
  local copies, waits for them, and re-layouts  29.9 us (11%)
  matrix products  28.6 us (11%)
  between operations  14 us (5%)
  starting transfers between devices  7.08 us (3%)
    reduce_scatter x1, waiting for transfers between devices, shards(): lax.psum_scatter(jnp.einsum('srd,vd->rsv', piece, w_proj, preferred_eleme...  37.4 us
    all_gather x1, waiting for transfers between devices, shards(): lax.all_gather(arrived, 'mp', axis=1, tiled=True)  24.3 us
    all_to_all x1, blocking collectives, shards(): lax.all_to_all(d_vis_slots[None], 'dp', split_axis=3, concat_axis=0, tile...  22.9 us
    all_to_all x1, blocking collectives, shards(): lax.all_to_all(vis_normed[None], 'dp', split_axis=2, concat_axis=0, tiled...  21.8 us
    all_to_all x1, blocking collectives, shards(): lax.all_to_all(packed, 'dp', split_axis=0, concat_axis=3, tiled=True)[0]  20 us
    unnamed x1, other arithmetic  18.6 us
    psum x1, blocking collectives, shards(): square_total = lax.psum(jnp.sum(embed_f * embed_f, axis=1), 'mp')  13.7 us
    unnamed x22, local copies, waits for them, and re-layouts  10.6 us
  transfers between devices with their start and end apart: 5, of which 3 were waited for; matrix products, arithmetic and copies ran while one was open for 24% of the time, Pallas kernels for 0%

commit v1 on v0

v1 whole, which is shorter than its diff:
```python
import jax
import jax.numpy as jnp
from jax import lax
from jax.experimental import pallas as pl
from jax.experimental.pallas import tpu as pltpu
from jax.sharding import PartitionSpec as P

D = 8192
DV = 3200
PATCH = 256
LANE = 128
CHUNK = 16
BF = jnp.bfloat16
F32 = jnp.float32
VMEM = pl.BlockSpec(memory_space=pltpu.VMEM)
SMEM = pl.BlockSpec(memory_space=pltpu.SMEM)

RING = 4
UP = [(2 * y + c, 2 * ((y + 1) % RING) + c) for y in range(RING) for c in range(2)]
DOWN = [(2 * y + c, 2 * ((y + 3) % RING) + c) for y in range(RING) for c in range(2)]
ACROSS = [(2 * y + c, 2 * ((y + 2) % RING) + c) for y in range(RING) for c in range(2)]
PEER = [(2 * y + c, 2 * y + 1 - c) for y in range(RING) for c in range(2)]


def up(x):
    return lax.ppermute(x, "mp", UP)


def down(x):
    return lax.ppermute(x, "mp", DOWN)


def across(x):
    return lax.ppermute(x, "mp", ACROSS)


def peer(x):
    return lax.ppermute(x, "mp", PEER)


def call(kernel, name, outs, args, scalars=0, scratch=(), flops=0, mib=40):
    size = sum(a.size * a.dtype.itemsize for a in args) + sum(o.size * o.dtype.itemsize for o in outs)
    return pl.pallas_call(
        kernel,
        in_specs=[SMEM] * scalars + [VMEM] * (len(args) - scalars),
        out_specs=[VMEM] * len(outs),
        out_shape=list(outs),
        scratch_shapes=list(scratch),
        compiler_params=pltpu.CompilerParams(vmem_limit_bytes=mib * 1024 * 1024),
        cost_estimate=pl.CostEstimate(flops=flops, bytes_accessed=size, transcendentals=0),
        name=name,
    )(*args)


def shape(dims, dtype):
    return jax.ShapeDtypeStruct(dims, dtype)


def dot(a, b):
    return jnp.dot(a, b, preferred_element_type=F32)


def dot_t(a, b):
    return lax.dot_general(a, b, (((1,), (1,)), ((), ())), preferred_element_type=F32)


def as_row(column):
    n = column.shape[0]
    return jnp.transpose(jnp.broadcast_to(column, (n, LANE)))[:1]


def as_column(row):
    n = row.shape[1]
    return jnp.transpose(jnp.broadcast_to(row, (LANE, n)))[:, :1]


def lane_block(ref, index, rows=slice(None)):
    return ref[rows, pl.ds(pl.multiple_of(index * LANE, LANE), LANE)]


def vision_norm(vision, gain):
    def kernel(v_ref, g_ref, o_ref, s_ref):
        v = v_ref[...].astype(F32)
        scale = lax.rsqrt(jnp.mean(v * v, axis=1, keepdims=True) + 1e-06)
        s_ref[...] = scale
        o_ref[...] = (v * scale * g_ref[...]).astype(BF)

    rows = vision.shape[0]
    return call(kernel, "vision_norm", [shape(vision.shape, BF), shape((rows, 1), F32)], [vision, gain])


def pack_grads(key_grad, value_grad):
    rows = key_grad.shape[0]
    slots = rows // PATCH
    per = PATCH // CHUNK

    def kernel(k_ref, v_ref, stack_ref, chunk_ref):
        stack_ref[:rows] = k_ref[...]
        stack_ref[rows:] = v_ref[...]
        for s in range(slots):
            for c in range(per):
                at = pl.ds(s * PATCH + c * CHUNK, CHUNK)
                chunk_ref[c, s] = k_ref[at]
                chunk_ref[per + c, s] = v_ref[at]

    return call(
        kernel,
        "pack_grads",
        [shape((2 * rows, LANE), BF), shape((2 * per, slots, CHUNK, LANE), BF)],
        [key_grad, value_grad],
    )


def take_blocks(index, x):
    count = index.shape[0]

    def kernel(index_ref, x_ref, o_ref):
        for j in range(count):
            o_ref[j] = x_ref[index_ref[j]]

    return call(kernel, "take_blocks", [shape((count,) + x.shape[1:], x.dtype)], [index, x], scalars=1)[0]


def text_forward(text, gain, w_key, w_value):
    rows, width = text.shape
    blocks = w_key.shape[1] // LANE

    def kernel(t_ref, g_ref, k_ref, v_ref, o_ref, q_ref, scaled):
        @pl.loop(0, rows // 64)
        def _(i):
            at = pl.ds(pl.multiple_of(i * 64, 64), 64)
            scaled[at] = (t_ref[at].astype(F32) * g_ref[...]).astype(BF)

        @pl.loop(0, rows // LANE)
        def _(i):
            t = t_ref[pl.ds(pl.multiple_of(i * LANE, LANE), LANE)].astype(F32)
            q_ref[pl.ds(i, 1)] = as_row(jnp.sum(t * t, axis=1, keepdims=True))

        @pl.loop(0, blocks)
        def _(b):
            w = jnp.concatenate([lane_block(k_ref, b), lane_block(v_ref, b)], axis=1)
            o_ref[b] = dot(scaled[...], w).astype(BF)

    return call(
        kernel,
        "text_forward",
        [shape((blocks, rows, 2 * LANE), BF), shape((rows // LANE, LANE), F32)],
        [text, gain, w_key, w_value],
        scratch=[pltpu.VMEM((rows, width), BF)],
        flops=4 * rows * width * w_key.shape[1],
    )


def image_forward(order, parts, w_proj, gain, w_key, w_value):
    pieces = [t for part in parts for t in part]
    starts = []
    for b, part in enumerate(parts):
        at = 0
        for t in part:
            starts.append((b, at))
            at += t.shape[0]
    rows_each = PATCH // len(parts)
    depth, width = w_proj.shape

    def kernel(order_ref, *refs):
        piece_refs = refs[: len(pieces)]
        p_ref, g_ref, k_ref, v_ref, e_ref, far_ref, near_ref, q_ref, vis, scaled = refs[len(pieces) :]
        for (b, at), ref in zip(starts, piece_refs):
            row = pl.multiple_of(order_ref[b] * rows_each + at, 16)
            vis[pl.ds(row, ref.shape[0])] = ref[...]

        @pl.loop(0, width // 256)
        def _(n):
            cols = pl.ds(pl.multiple_of(n * 256, 256), 256)
            e_ref[:, cols] = dot(vis[...], p_ref[:, cols]).astype(BF)

        @pl.loop(0, PATCH // LANE)
        def _(i):
            at = pl.ds(pl.multiple_of(i * LANE, LANE), LANE)
            e = e_ref[at].astype(F32)
            scaled[at] = (e * g_ref[...]).astype(BF)
            q_ref[pl.ds(i, 1)] = as_row(jnp.sum(e * e, axis=1, keepdims=True))

        @pl.loop(0, RING)
        def _(b):
            there = order_ref[RING + b]
            w = jnp.concatenate([lane_block(k_ref, there), lane_block(v_ref, there)], axis=1)
            far_ref[b] = dot(scaled[...], w).astype(BF)
            own = order_ref[b]
            w = jnp.concatenate([lane_block(k_ref, own), lane_block(v_ref, own)], axis=1)
            near_ref[b] = dot(scaled[...], w)

    return call(
        kernel,
        "image_forward",
        [
            shape((PATCH, width), BF),
            shape((RING, PATCH, 2 * LANE), BF),
            shape((RING, PATCH, 2 * LANE), F32),
            shape((PATCH // LANE, LANE), F32),
        ],
        [order, *pieces, w_proj, gain, w_key, w_value],
        scalars=1,
        scratch=[pltpu.VMEM((PATCH, depth), BF), pltpu.VMEM((PATCH, width), BF)],
        flops=2 * PATCH * width * (depth + 2 * w_key.shape[1]),
    )


def backward(order, pieces, w_key, w_value, gain, embed):
    rows, width = embed.shape
    cols = w_key.shape[1]

    def kernel(order_ref, *refs):
        piece_refs = refs[: len(pieces)]
        k_ref, v_ref, g_ref, e_ref, d_ref, i_ref, gk, gv = refs[len(pieces) :]
        b = 0
        for ref in piece_refs:
            for j in range(ref.shape[0] // (2 * rows)):
                at = pl.ds(pl.multiple_of(order_ref[b] * LANE, LANE), LANE)
                gk[:, at] = ref[2 * rows * j : 2 * rows * j + rows]
                gv[:, at] = ref[2 * rows * j + rows : 2 * rows * (j + 1)]
                b += 1

        @pl.loop(0, width // 256)
        def _(n):
            at = pl.ds(pl.multiple_of(n * 256, 256), 256)
            d = dot_t(gk[...], k_ref[at]) + dot_t(gv[...], v_ref[at])
            d_ref[:, at] = d * g_ref[:, at]

        @pl.loop(0, rows // LANE)
        def _(i):
            at = pl.ds(pl.multiple_of(i * LANE, LANE), LANE)
            i_ref[pl.ds(i, 1)] = as_row(jnp.sum(d_ref[at] * e_ref[at].astype(F32), axis=1, keepdims=True))

    return call(
        kernel,
        "backward",
        [shape((rows, width), F32), shape((rows // LANE, LANE), F32)],
        [order, *pieces, w_key, w_value, gain, embed],
        scalars=1,
        scratch=[pltpu.VMEM((rows, cols), BF), pltpu.VMEM((rows, cols), BF)],
        flops=4 * rows * width * cols,
    )


def embed_grad(d, e, square_row, inner_row):
    scale = lax.rsqrt(as_column(square_row) / D + 1e-05)
    inner = as_column(inner_row) / D
    return scale * d - e * (scale * scale * scale * inner)


def image_backward(order, image_d, embed, square, inner, w_proj):
    depth, width = w_proj.shape
    rows_each = PATCH // 8
    half = PATCH // 2
    cut = 640

    def kernel(order_ref, d_ref, e_ref, q_ref, i_ref, p_ref, far_ref, near_ref, grad, turned):
        @pl.loop(0, PATCH // LANE)
        def _(i):
            at = pl.ds(pl.multiple_of(i * LANE, LANE), LANE)
            row = pl.ds(i, 1)
            grad[at] = embed_grad(d_ref[at], e_ref[at].astype(F32), q_ref[row], i_ref[row]).astype(BF)

        for b in range(8):
            at = pl.ds(pl.multiple_of(order_ref[b] * rows_each, rows_each), rows_each)
            turned[b * rows_each : (b + 1) * rows_each] = grad[at]

        @pl.loop(0, depth // cut)
        def _(n):
            at = pl.ds(pl.multiple_of(n * cut, LANE), cut)
            r = dot_t(turned[...], p_ref[at])
            near_ref[:, at] = r[:half]
            far_ref[:, at] = r[half:].astype(BF)

    return call(
        kernel,
        "image_backward",
        [shape((half, depth), BF), shape((half, depth), F32)],
        [order, image_d, embed, square, inner, w_proj],
        scalars=1,
        scratch=[pltpu.VMEM((PATCH, width), BF), pltpu.VMEM((PATCH, width), BF)],
        flops=2 * PATCH * width * depth,
    )


def ring_first(near, other):
    _, n, c = near.shape
    h = n // 2

    def kernel(a_ref, b_ref, up_ref, down_ref, here_ref, above_ref, below_ref):
        def total(k, at):
            return a_ref[k, at] + b_ref[k, at].astype(F32)

        first, second = slice(0, h), slice(h, n)
        up_ref[first] = total(2, first).astype(BF)
        up_ref[second] = total(1, second).astype(BF)
        down_ref[first] = total(3, first).astype(BF)
        down_ref[second] = total(2, second).astype(BF)
        here_ref[...] = total(0, slice(0, n))
        above_ref[...] = total(1, first)
        below_ref[...] = total(3, second)

    return call(
        kernel,
        "ring_first",
        [shape((n, c), BF), shape((n, c), BF), shape((n, c), F32), shape((h, c), F32), shape((h, c), F32)],
        [near, other],
    )


def ring_sum(near, far):
    up1, down1, here, above, below = ring_first(near, peer(far).reshape(near.shape))
    h = above.shape[0]
    up1, down1 = up(up1), down(down1)
    up2 = up((above + up1[:h].astype(F32)).astype(BF))
    down2 = down((below + down1[h:].astype(F32)).astype(BF))
    return here, up1, down1, up2, down2


def ring_total(here_ref, up1_ref, down1_ref, up2_ref, down2_ref):
    h = up2_ref.shape[0]
    first = here_ref[:h] + down1_ref[:h].astype(F32) + up2_ref[...].astype(F32)
    second = here_ref[h:] + up1_ref[h:].astype(F32) + down2_ref[...].astype(F32)
    return first, second


def image_out(pieces, square):
    h = PATCH // 2

    def kernel(*refs):
        q_ref, o_ref = refs[5:]
        for j, t in enumerate(ring_total(*refs[:5])):
            scale = lax.rsqrt(as_column(q_ref[j : j + 1]) / D + 1e-05)
            t = (t * scale).astype(BF)
            o_ref[j * h : (j + 1) * h] = t[:, :LANE]
            o_ref[PATCH + j * h : PATCH + (j + 1) * h] = t[:, LANE:]

    return call(kernel, "image_out", [shape((2 * PATCH, LANE), BF)], [*pieces, square])[0]


def vision_out(pieces, vision, gain, scale):
    rows = vision.shape[0]
    h = rows // 2

    def kernel(*refs):
        v_ref, g_ref, s_ref, o_ref = refs[5:]
        for j, t in enumerate(ring_total(*refs[:5])):
            at = slice(j * h, (j + 1) * h)
            v, s = v_ref[at].astype(F32), s_ref[at]
            grad_h = t.astype(BF).astype(F32) * g_ref[...]
            inner = jnp.mean(grad_h * v, axis=1, keepdims=True)
            o_ref[at] = (s * grad_h - v * (s * s * s * inner)).astype(BF)

    return call(kernel, "vision_out", [shape(vision.shape, BF)], [*pieces, vision, gain, scale])[0]


def text_out(filled, text_d, text, square, inner):
    rows, width = text.shape

    def kernel(f_ref, d_ref, t_ref, q_ref, i_ref, o_ref):
        @pl.loop(0, rows // LANE)
        def _(i):
            at = pl.ds(pl.multiple_of(i * LANE, LANE), LANE)
            row = pl.ds(i, 1)
            grad = embed_grad(d_ref[at], t_ref[at].astype(F32), q_ref[row], i_ref[row])
            o_ref[at] = jnp.where(f_ref[i // (PATCH // LANE)] > 0, 0.0, grad).astype(BF)

    return call(
        kernel, "text_out", [shape((rows, width), BF)], [filled, text_d, text, square, inner], scalars=1
    )[0]


def key_value_out(filled, text_kv, square, arrived):
    rows = text_kv.shape[0]
    per = PATCH // CHUNK

    def kernel(f_ref, t_ref, q_ref, a_ref, k_ref, v_ref):
        for s in range(rows // PATCH):
            @pl.when(f_ref[s] > 0)
            def _():
                for c in range(per):
                    at = pl.ds(s * PATCH + c * CHUNK, CHUNK)
                    k_ref[at] = a_ref[c, s]
                    v_ref[at] = a_ref[per + c, s]

            @pl.when(f_ref[s] == 0)
            def _():
                for i in range(PATCH // LANE):
                    j = s * (PATCH // LANE) + i
                    at = pl.ds(j * LANE, LANE)
                    scale = lax.rsqrt(as_column(q_ref[j : j + 1]) / D + 1e-05)
                    t = (t_ref[at].astype(F32) * scale).astype(BF)
                    k_ref[at] = t[:, :LANE]
                    v_ref[at] = t[:, LANE:]

    return call(
        kernel,
        "key_value_out",
        [shape((rows, LANE), BF), shape((rows, LANE), BF)],
        [filled, text_kv, square, arrived],
        scalars=1,
    )


def ring_gather(x):
    half = x.shape[0] // 2
    below, above = up(x), down(x)
    far = [up(below[:half]), down(above[half:])]
    mine = [[x], [above], far, [below]]
    other = [[peer(t) for t in part] for part in mine]
    return mine + other


def short_gather(x):
    mine = [x, down(x), across(x), up(x)]
    return mine + [peer(t) for t in mine]


def small_sum(x):
    pair = x + peer(x)
    return (pair + up(pair)) + (down(pair) + across(pair))


def shards(
    vision,
    vision_gain,
    image_slot,
    text_embed,
    w_proj,
    llm_gain,
    w_key,
    w_value,
    key_grad,
    value_grad,
):
    dp = lax.axis_size("dp")
    here = lax.axis_index("dp")
    m = lax.axis_index("mp")
    y, c = m // 2, m % 2
    slots = text_embed.shape[0] // PATCH
    text_rows = text_embed.shape[0] // LANE

    rel = jnp.arange(8, dtype=jnp.int32)
    order = ((y + rel % RING) % RING) * 2 + (c ^ (rel // RING))
    slot_ids = jnp.arange(dp * slots, dtype=jnp.int32)
    onehot = slot_ids[:, None] == image_slot[None, :]
    owner = jnp.sum(jnp.where(onehot, jnp.arange(dp, dtype=jnp.int32)[None, :], 0), axis=1)
    mine = slot_ids[:slots] + here * slots
    filled = jnp.any(mine[:, None] == image_slot[None, :], axis=1).astype(jnp.int32)
    gain = llm_gain[None]
    vis_gain = vision_gain[None]

    vis_normed, vis_scale = vision_norm(vision, vis_gain)
    with jax.named_scope("vision_gather"):
        vis_parts = ring_gather(vis_normed)

    grad_stack, grad_chunks = pack_grads(key_grad, value_grad)
    with jax.named_scope("text_grad_gather"):
        text_g = lax.all_gather(grad_stack, "mp", axis=0, tiled=True)
    with jax.named_scope("slot_grads_spread"):
        spread = lax.all_to_all(grad_chunks, "dp", split_axis=0, concat_axis=0, tiled=True)
    picked = take_blocks(image_slot, spread.reshape(dp * slots, CHUNK, LANE))
    with jax.named_scope("slot_grads_collect"):
        image_kv_grad = lax.all_to_all(picked, "dp", split_axis=0, concat_axis=0, tiled=True)
    with jax.named_scope("image_grad_gather"):
        image_g = short_gather(image_kv_grad.reshape(2 * PATCH, LANE))

    text_part, text_square = text_forward(text_embed, gain, w_key, w_value)
    with jax.named_scope("text_key_value_sum"):
        text_kv = lax.psum_scatter(text_part, "mp", scatter_dimension=0, tiled=False)

    embed, far, near, image_square = image_forward(order, vis_parts, w_proj, gain, w_key, w_value)
    with jax.named_scope("image_key_value_sum"):
        pieces = ring_sum(near, far)
    with jax.named_scope("squares_sum"):
        squares = small_sum(jnp.concatenate([text_square, image_square]))
    text_square, image_square = squares[:text_rows], squares[text_rows:]

    image_kv = image_out(pieces, image_square).reshape(dp, CHUNK, LANE)
    with jax.named_scope("image_out_spread"):
        spread = lax.all_to_all(image_kv, "dp", split_axis=0, concat_axis=0, tiled=True)
    packed = take_blocks(owner, spread).reshape(dp, slots, CHUNK, LANE)
    with jax.named_scope("image_out_collect"):
        arrived = lax.all_to_all(packed, "dp", split_axis=0, concat_axis=0, tiled=True)

    text_d, text_inner = backward(rel, [text_g], w_key, w_value, gain, text_embed)
    image_d, image_inner = backward(order, image_g, w_key, w_value, gain, embed)
    with jax.named_scope("inner_sum"):
        inner = small_sum(jnp.concatenate([text_inner, image_inner]))
    d_far, d_near = image_backward(order, image_d, embed, image_square, inner[text_rows:], w_proj)
    with jax.named_scope("d_vis_sum"):
        d_pieces = ring_sum(d_near.reshape(RING, -1, DV), d_far)
    vision_grad = vision_out(d_pieces, vision, vis_gain, vis_scale)
    text_grad = text_out(filled, text_d, text_embed, text_square, inner[:text_rows])
    key_out, value_out = key_value_out(filled, text_kv, text_square, arrived)
    return key_out, value_out, text_grad, vision_grad


def solution(mesh):
    placed = (
        P(("dp", "mp"), None),
        P(),
        P(),
        P("dp", "mp"),
        P(None, "mp"),
        P("mp"),
        P("mp", None),
        P("mp", None),
        P("dp", "mp"),
        P("dp", "mp"),
    )
    return jax.shard_map(
        shards,
        mesh=mesh,
        in_specs=placed,
        out_specs=(P("dp", "mp"), P("dp", "mp"), P("dp", "mp"), P(("dp", "mp"), None)),
        check_vma=False,
    )
```

time: 263 us -> 192 us (0.73)
  blocking collectives: 78.3 us -> 0 us
  starting transfers between devices: 7.08 us -> 67.7 us
  waiting for transfers between devices: 70 us -> 27.4 us
  Pallas kernels: 0 us -> 36.1 us
  matrix products: 28.6 us -> 0 us
  other arithmetic: 32.4 us -> 4.88 us
  local copies, waits for them, and re-layouts: 29.9 us -> 40.4 us
    all_to_all x3 -> x0, blocking collectives: 64.7 us -> none  [the longest x1 22.9 us: shards(): lax.all_to_all(d_vis_slots[None], 'dp', split_axis=3, concat_axis=0, tile...]
    reduce_scatter x2 -> x1, waiting for transfers between devices: 37.4 us -> 0.01 us  [shards(): lax.psum_scatter(text_part, 'mp', scatter_dimension=0, tiled=False)]
    pallas_call x0 -> x15, Pallas kernels: none -> 36.1 us  [call(): pl.pallas_call(kernel, in_specs=[SMEM] * scalars + [VMEM] * (len(args) -...]
    ppermute x0 -> x34, starting transfers between devices: none -> 35.7 us  [the longest x9 26.8 us: down(): return lax.ppermute(x, 'mp', DOWN)]
    dot_general x8 -> x0, matrix products: 28.6 us -> none  [the longest x1 8.56 us: shards(): jnp.einsum('srd,vd->rsv', piece, w_proj, preferred_element_type=jnp.float32)]
    unnamed x22 -> x122, local copies, waits for them, and re-layouts: 10.6 us -> 39 us
    all_to_all x1 -> x4, starting transfers between devices: 6.51 us -> 32 us  [the longest x1 11.6 us: shards(): lax.all_to_all(grad_chunks, 'dp', split_axis=0, concat_axis=0, tiled=True)]
    all_gather x2 -> x1, waiting for transfers between devices: 24.3 us -> 0.01 us  [shards(): text_g = lax.all_gather(grad_stack, 'mp', axis=0, tiled=True)]
  transfers between devices with their start and end apart: 5 -> 40, of which waited for: 3 -> 11; matrix products, arithmetic and copies ran while one was open for 24% -> 3% of each run, Pallas kernels for 0% -> 17%
where the time goes in v1:
time: 192 us; the launch traced here: 191 us
  starting transfers between devices  67.7 us (35%)
  local copies, waits for them, and re-layouts  40.4 us (21%)
  Pallas kernels  36.1 us (19%)
  waiting for transfers between devices  27.4 us (14%)
  between operations  14.6 us (8%)
  other arithmetic  4.88 us (3%)
    unnamed x122, local copies, waits for them, and re-layouts  39 us
    pallas_call x15, Pallas kernels, call(): pl.pallas_call(kernel, in_specs=[SMEM] * scalars + [VMEM] * (len(args) -...  36.1 us
    ppermute x9, starting transfers between devices, down(): return lax.ppermute(x, 'mp', DOWN)  26.8 us
    all_to_all x1, starting transfers between devices, shards(): lax.all_to_all(grad_chunks, 'dp', split_axis=0, concat_axis=0, tiled=True)  11.6 us
    ppermute x9, waiting for transfers between devices, up(): return lax.ppermute(x, 'mp', UP)  9.19 us
    all_to_all x1, starting transfers between devices, shards(): lax.all_to_all(image_kv, 'dp', split_axis=0, concat_axis=0, tiled=True)  7.67 us
    all_to_all x1, starting transfers between devices, shards(): lax.all_to_all(packed, 'dp', split_axis=0, concat_axis=0, tiled=True)  7.13 us
    all_to_all x1, waiting for transfers between devices, shards(): lax.all_to_all(grad_chunks, 'dp', split_axis=0, concat_axis=0, tiled=True)  6.34 us
  transfers between devices with their start and end apart: 40, of which 11 were waited for; matrix products, arithmetic and copies ran while one was open for 3% of the time, Pallas kernels for 17%

profile of v1, /device:TPU:2, one launch (start us, length us, event | category | flops | bytes accessed | tf_op | source)
XLA Modules:
  0.0 191.0 jit_solution(16483263609507920513)
XLA Ops:
  10.1 11.6 %all-to-all-start.2 = ((bf16[32,2,16,128]{3,2,1,0:T(8,128)(2,1)}), bf16[32,2,16,128]{3,2,1,0:T(8,128)(2,1)S(1)}, u32[]{:S(2)}, u32[]{:S(2)}) async-start(bf16[32,2,16,128]{3,2,1,0:T(8,128)(2,1)} %get-tuple-element.48), calls=%async_computation.3 | async-start | bytes 524288 | tf_op jit(solution)/shard_map/slot_grads_spread/all_to_all | solution.py:462
  23.5 3.1 %collective-permute-start = (bf16[32,3200]{1,0:T(8,128)(2,1)S(1)}, bf16[32,3200]{1,0:T(8,128)(2,1)S(1)}, u32[]{:S(2)}, u32[]{:S(2)}) collective-permute-start(bf16[32,3200]{1,0:T(8,128)(2,1)S(1)} %get-tuple-element.34.refs_0_), channel_id=1, source_target_pairs={{0,6},{1,7},{2,0},{3,1},{4,2},{5,3},{6,4},{7,5},{8,14},{9,15},{10,... | collective-permute-start | bytes 614408 | tf_op jit(solution)/shard_map/vision_gather/ppermute | solution.py:30
  26.6 6.3 %all-to-all-done.2 = bf16[32,2,16,128]{3,2,1,0:T(8,128)(2,1)S(1)} async-done(((bf16[32,2,16,128]{3,2,1,0:T(8,128)(2,1)}), bf16[32,2,16,128]{3,2,1,0:T(8,128)(2,1)S(1)}, u32[]{:S(2)}, u32[]{:S(2)}) %all-to-all-start.2) | async-done | bytes 262176 | tf_op jit(solution)/shard_map/slot_grads_spread/all_to_all | solution.py:462
  34.9 5.6 %all-to-all-start.3 = ((bf16[32,16,128]{2,1,0:T(8,128)(2,1)}), bf16[32,16,128]{2,1,0:T(8,128)(2,1)S(1)}, u32[]{:S(2)}, u32[]{:S(2)}) async-start(bf16[32,16,128]{2,1,0:T(8,128)(2,1)} %take_blocks.3), calls=%async_computation.4 | async-start | bytes 262144 | tf_op jit(solution)/shard_map/slot_grads_collect/all_to_all | solution.py:465
  45.1 2.3 %collective-permute-done.2.refs_2_ = bf16[16,3200]{1,0:T(8,128)(2,1)S(1)} collective-permute-done((bf16[16,3200]{1,0:T(8,128)(2,1)S(1)}, bf16[16,3200]{1,0:T(8,128)(2,1)S(1)}, u32[]{:S(2)}, u32[]{:S(2)}) %collective-permute-start.2) | collective-permute-done | bytes 102432 | tf_op jit(solution)/shard_map/vision_gather/ppermute | solution.py:26
  47.4 2.3 %all-to-all-done.3 = bf16[32,16,128]{2,1,0:T(8,128)(2,1)S(1)} async-done(((bf16[32,16,128]{2,1,0:T(8,128)(2,1)}), bf16[32,16,128]{2,1,0:T(8,128)(2,1)S(1)}, u32[]{:S(2)}, u32[]{:S(2)}) %all-to-all-start.3) | async-done | bytes 131104 | tf_op jit(solution)/shard_map/slot_grads_collect/all_to_all | solution.py:465
  49.6 3.0 %collective-permute-start.18 = (bf16[512,128]{1,0:T(8,128)(2,1)S(1)}, bf16[512,128]{1,0:T(8,128)(2,1)}, u32[]{:S(2)}, u32[]{:S(2)}) collective-permute-start(bf16[512,128]{1,0:T(8,128)(2,1)S(1)} %bitcast.14), channel_id=1, source_target_pairs={{0,6},{1,7},{2,0},{3,1},{4,2},{5,3},{6,4},{7,5},{8,14},{9,15},{10,... | collective-permute-start | bytes 393224 | tf_op jit(solution)/shard_map/image_grad_gather/ppermute | solution.py:30
  57.8 4.8 %text_forward.1 = (bf16[8,512,256]{2,1,0:T(8,128)(2,1)S(1)}, f32[4,128]{1,0:T(4,128)S(1)}) custom-call(bf16[512,1024]{1,0:T(8,128)(2,1)S(1)} %copy-done.12, f32[1,1024]{1,0:T(1,128)S(1)} %bitcast.20, bf16[1024,1024]{1,0:T(8,128)(2,1)S(1)} %copy-done.1, bf16[1024,1024]{1,0:T(8,128)(2,1)S(1)} %copy-done.4), custom_call_target="tpu_custom_call" | custom-call | flops 2147483648 | bytes 7346176 | tf_op jit(solution)/shard_map/text_forward/pallas_call | solution.py:43
  66.5 2.9 %copy-done = bf16[3200,1024]{1,0:T(8,128)(2,1)S(1)} copy-done((bf16[3200,1024]{1,0:T(8,128)(2,1)S(1)}, bf16[3200,1024]{1,0:T(8,128)(2,1)}, u32[]{:S(2)}) %copy-start) | copy-done | bytes 6553624
  73.7 7.1 %image_forward.1 = (bf16[256,1024]{1,0:T(8,128)(2,1)S(1)}, bf16[4,256,256]{2,1,0:T(8,128)(2,1)}, f32[4,256,256]{2,1,0:T(8,128)S(1)}, f32[2,128]{1,0:T(2,128)S(1)}) custom-call(s32[8]{0:T(128)S(1)} %fusion.2.order_ref, bf16[32,3200]{1,0:T(8,128)(2,1)S(1)} %copy-done.32, bf16[32,3200]{1,0:T(8,128)(2,1)S(1)} %collective-permute-done.refs_1_, ...), custom_call_target="tpu_custom_call" | custom-call | flops 2751463424 | bytes 14488608 | tf_op jit(solution)/shard_map/image_forward/pallas_call | solution.py:43
  83.7 3.8 %backward.3 = (f32[256,1024]{1,0:T(8,128)S(1)}, f32[2,128]{1,0:T(2,128)S(1)}) custom-call(s32[8]{0:T(128)S(1)} %fusion.2.order_ref, bf16[512,128]{1,0:T(8,128)(2,1)S(1)} %bitcast.18, bf16[512,128]{1,0:T(8,128)(2,1)} %collective-permute-done.18.refs_1_, bf16[512,128]{1,0:T(8,128)(2,1)} %collective-permute-done.19.refs_2_, ...), custom_call_target="tpu_custom_call" | custom-call | flops 1073741824 | bytes 6820896 | tf_op jit(solution)/shard_map/backward/pallas_call | solution.py:43
  95.7 4.8 %backward.2 = (f32[512,1024]{1,0:T(8,128)S(1)}, f32[4,128]{1,0:T(4,128)S(1)}) custom-call(s32[8]{0:T(128)S(1)} %iota.20.order_ref, bf16[8192,128]{1,0:T(8,128)(2,1)S(1)} %copy-done.57, bf16[1024,1024]{1,0:T(8,128)(2,1)S(1)} %copy-done.3, bf16[1024,1024]{1,0:T(8,128)(2,1)S(1)} %copy-done.6, f32[1,1024]{1,0:T(1,128)S(1)} %bitcast.23, ...), custom_call_target="tpu_custom_call" | custom-call | flops 2147483648 | bytes 9443360 | tf_op jit(solution)/shard_map/backward/pallas_call | solution.py:43
  106.9 3.3 %collective-permute-start.27 = (f32[6,128]{1,0:T(8,128)S(1)}, f32[6,128]{1,0:T(8,128)S(1)}, u32[]{:S(2)}, u32[]{:S(2)}) collective-permute-start(f32[6,128]{1,0:T(8,128)S(1)} %fusion.5), channel_id=1, source_target_pairs={{0,6},{1,7},{2,0},{3,1},{4,2},{5,3},{6,4},{7,5},{8,14},{9,15},{10,... | collective-permute-start | bytes 9224 | tf_op jit(solution)/shard_map/inner_sum/ppermute | solution.py:30
  111.7 3.6 %collective-permute-done.28 = f32[6,128]{1,0:T(8,128)S(1)} collective-permute-done((f32[6,128]{1,0:T(8,128)S(1)}, f32[6,128]{1,0:T(8,128)S(1)}, u32[]{:S(2)}, u32[]{:S(2)}) %collective-permute-start.28) | collective-permute-done | bytes 3104 | tf_op jit(solution)/shard_map/inner_sum/ppermute | solution.py:34
  115.8 5.0 %image_backward.1 = (bf16[128,3200]{1,0:T(8,128)(2,1)}, f32[128,3200]{1,0:T(8,128)S(1)}) custom-call(s32[8]{0:T(128)S(1)} %copy-done.50, f32[256,1024]{1,0:T(8,128)S(1)} %copy-done.16, bf16[256,1024]{1,0:T(8,128)(2,1)S(1)} %get-tuple-element.49.refs_11_.e_ref, f32[2,128]{1,0:T(2,128)S(1)} %slice.39.refs_5_.q_ref, f32[2,128]{1,0:T(2,128)S(1)} %slice.41.i_ref, ...), custom_call_target="tpu_custom_call" | custom-call | flops 1677721600 | bytes 10586144 | tf_op jit(solution)/shard_map/image_backward/pallas_call | solution.py:43
  122.2 3.2 %collective-permute-start.15 = (bf16[256,256]{1,0:T(8,128)(2,1)S(1)}, bf16[256,256]{1,0:T(8,128)(2,1)S(1)}, u32[]{:S(2)}, u32[]{:S(2)}) collective-permute-start(bf16[256,256]{1,0:T(8,128)(2,1)S(1)} %get-tuple-element.40), channel_id=1, source_target_pairs={{0,6},{1,7},{2,0},{3,1},{4,2},{5,3},{6,4},{7,5},{8,14},{9,15},{10,... | collective-permute-start | bytes 393224 | tf_op jit(solution)/shard_map/image_key_value_sum/ppermute | solution.py:30
  125.4 3.9 %collective-permute-done.14.refs_1_ = bf16[256,256]{1,0:T(8,128)(2,1)S(1)} collective-permute-done((bf16[256,256]{1,0:T(8,128)(2,1)S(1)}, bf16[256,256]{1,0:T(8,128)(2,1)S(1)}, u32[]{:S(2)}, u32[]{:S(2)}) %collective-permute-start.14) | collective-permute-done | bytes 131104 | tf_op jit(solution)/shard_map/image_key_value_sum/ppermute | solution.py:26
  129.7 3.3 %collective-permute-start.17 = (bf16[128,256]{1,0:T(8,128)(2,1)S(1)}, bf16[128,256]{1,0:T(8,128)(2,1)S(1)}, u32[]{:S(2)}, u32[]{:S(2)}) collective-permute-start(bf16[128,256]{1,0:T(8,128)(2,1)S(1)} %add_convert_fusion.2), channel_id=1, source_target_pairs={{0,6},{1,7},{2,0},{3,1},{4,2},{5,3},{6,4},{7,5},{8,14},{9,15},{10,... | collective-permute-start | bytes 196616 | tf_op jit(solution)/shard_map/image_key_value_sum/ppermute | solution.py:30
  136.0 7.7 %all-to-all-start = ((bf16[32,16,128]{2,1,0:T(8,128)(2,1)}), bf16[32,16,128]{2,1,0:T(8,128)(2,1)S(1)}, u32[]{:S(2)}, u32[]{:S(2)}) async-start(bf16[32,16,128]{2,1,0:T(8,128)(2,1)} %bitcast.2), calls=%async_computation.1 | async-start | bytes 262144 | tf_op jit(solution)/shard_map/image_out_spread/all_to_all | solution.py:482
  150.2 2.7 %all-to-all-done.x_ref = bf16[32,16,128]{2,1,0:T(8,128)(2,1)S(1)} async-done(((bf16[32,16,128]{2,1,0:T(8,128)(2,1)}), bf16[32,16,128]{2,1,0:T(8,128)(2,1)S(1)}, u32[]{:S(2)}, u32[]{:S(2)}) %all-to-all-start) | async-done | bytes 131104 | tf_op jit(solution)/shard_map/image_out_spread/all_to_all | solution.py:482
  154.2 7.1 %all-to-all-start.1 = ((bf16[32,2,16,128]{3,2,1,0:T(8,128)(2,1)}), bf16[32,2,16,128]{3,2,1,0:T(8,128)(2,1)S(1)}, u32[]{:S(2)}, u32[]{:S(2)}) async-start(bf16[32,2,16,128]{3,2,1,0:T(8,128)(2,1)} %bitcast.11), calls=%async_computation.2 | async-start | bytes 524288 | tf_op jit(solution)/shard_map/image_out_collect/all_to_all | solution.py:485
  161.3 3.4 %collective-permute-start.31 = (bf16[32,3200]{1,0:T(8,128)(2,1)}, bf16[32,3200]{1,0:T(8,128)(2,1)S(1)}, u32[]{:S(2)}, u32[]{:S(2)}) collective-permute-start(bf16[32,3200]{1,0:T(8,128)(2,1)} %copy-done.58), channel_id=1, source_target_pairs={{0,6},{1,7},{2,0},{3,1},{4,2},{5,3},{6,4},{7,5},{8,14},{9,15},{10,... | collective-permute-start | bytes 614408 | tf_op jit(solution)/shard_map/d_vis_sum/ppermute | solution.py:30
  170.6 3.6 %collective-permute-start.33 = (bf16[16,3200]{1,0:T(8,128)(2,1)}, bf16[16,3200]{1,0:T(8,128)(2,1)}, u32[]{:S(2)}, u32[]{:S(2)}) collective-permute-start(bf16[16,3200]{1,0:T(8,128)(2,1)} %add_convert_fusion), channel_id=1, source_target_pairs={{0,6},{1,7},{2,0},{3,1},{4,2},{5,3},{6,4},{7,5},{8,14},{9,15},{10,... | collective-permute-start | bytes 307208 | tf_op jit(solution)/shard_map/d_vis_sum/ppermute | solution.py:30
  174.4 2.5 %text_out.1 = bf16[512,1024]{1,0:T(8,128)(2,1)} custom-call(s32[2]{0:T(128)S(1)} %convert_element_type.27.f_ref, f32[512,1024]{1,0:T(8,128)S(1)} %copy-done.8, bf16[512,1024]{1,0:T(8,128)(2,1)S(1)} %copy-done.14, f32[4,128]{1,0:T(4,128)S(1)} %slice.36.q_ref, f32[4,128]{1,0:T(4,128)S(1)} %slice.40.i_ref), custom_call_target="tpu_custom_call" | custom-call | bytes 4198408 | tf_op jit(solution)/shard_map/text_out/pallas_call | solution.py:43
  (220 shorter events, 69.6 us)
Async XLA Ops:
  7.2 81.8 %all-gather.2.cloned.1.call-start = ((), (), s32[]{:S(2)}) async-start(), calls=%async_computation.6 | async-start | bytes 2359296 | tf_op jit(solution)/shard_map/text_grad_gather/all_gather | solution.py:460
  10.1 22.9 %all-to-all-start.2 = ((bf16[32,2,16,128]{3,2,1,0:T(8,128)(2,1)}), bf16[32,2,16,128]{3,2,1,0:T(8,128)(2,1)S(1)}, u32[]{:S(2)}, u32[]{:S(2)}) async-start(bf16[32,2,16,128]{3,2,1,0:T(8,128)(2,1)} %get-tuple-element.48), calls=%async_computation.3 | async-start | bytes 524288 | tf_op jit(solution)/shard_map/slot_grads_spread/all_to_all | solution.py:462
  23.5 17.1 %collective-permute-start = (bf16[32,3200]{1,0:T(8,128)(2,1)S(1)}, bf16[32,3200]{1,0:T(8,128)(2,1)S(1)}, u32[]{:S(2)}, u32[]{:S(2)}) collective-permute-start(bf16[32,3200]{1,0:T(8,128)(2,1)S(1)} %get-tuple-element.34.refs_0_), channel_id=1, source_target_pairs={{0,6},{1,7},{2,0},{3,1},{4,2},{5,3},{6,4},{7,5},{8,14},{9,15},{10,... | collective-permute-start | bytes 614408 | tf_op jit(solution)/shard_map/vision_gather/ppermute | solution.py:30
  26.6 14.5 %collective-permute-start.1 = (bf16[32,3200]{1,0:T(8,128)(2,1)S(1)}, bf16[32,3200]{1,0:T(8,128)(2,1)S(1)}, u32[]{:S(2)}, u32[]{:S(2)}) collective-permute-start(bf16[32,3200]{1,0:T(8,128)(2,1)S(1)} %get-tuple-element.34.refs_0_), channel_id=1, source_target_pairs={{0,2},{1,3},{2,4},{3,5},{4,6},{5,7},{6,0},{7,1},{8,10},{9,11},{10,... | collective-permute-start | bytes 614408 | tf_op jit(solution)/shard_map/vision_gather/ppermute | solution.py:26
  34.9 14.8 %all-to-all-start.3 = ((bf16[32,16,128]{2,1,0:T(8,128)(2,1)}), bf16[32,16,128]{2,1,0:T(8,128)(2,1)S(1)}, u32[]{:S(2)}, u32[]{:S(2)}) async-start(bf16[32,16,128]{2,1,0:T(8,128)(2,1)} %take_blocks.3), calls=%async_computation.4 | async-start | bytes 262144 | tf_op jit(solution)/shard_map/slot_grads_collect/all_to_all | solution.py:465
  40.4 136.4 %reduce-scatter.2.cloned.1.call-start = ((), (), s32[]{:S(2)}) async-start(), calls=%async_computation.5 | async-start | bytes 2359296 | tf_op jit(solution)/shard_map/text_key_value_sum/reduce_scatter | solution.py:471
  40.6 12.7 %collective-permute-start.5 = (bf16[32,3200]{1,0:T(8,128)(2,1)S(1)}, bf16[32,3200]{1,0:T(8,128)(2,1)S(1)}, u32[]{:S(2)}, u32[]{:S(2)}) collective-permute-start(bf16[32,3200]{1,0:T(8,128)(2,1)S(1)} %collective-permute-done.refs_1_), channel_id=1, source_target_pairs={{0,1},{1,0},{2,3},{3,2},{4,5},{5,4},{6,7},{7,6},{8,9},{9,8},{10,11... | collective-permute-start | bytes 614408 | tf_op jit(solution)/shard_map/vision_gather/ppermute | solution.py:38
  43.4 9.3 %collective-permute-start.3 = (bf16[16,3200]{1,0:T(8,128)(2,1)}, bf16[16,3200]{1,0:T(8,128)(2,1)S(1)}, u32[]{:S(2)}, u32[]{:S(2)}) collective-permute-start(bf16[16,3200]{1,0:T(8,128)(2,1)} %slice.45), channel_id=1, source_target_pairs={{0,6},{1,7},{2,0},{3,1},{4,2},{5,3},{6,4},{7,5},{8,14},{9,15},{10,... | collective-permute-start | bytes 307208 | tf_op jit(solution)/shard_map/vision_gather/ppermute | solution.py:30
  45.1 21.4 %collective-permute-start.8 = (bf16[32,3200]{1,0:T(8,128)(2,1)S(1)}, bf16[32,3200]{1,0:T(8,128)(2,1)}, u32[]{:S(2)}, u32[]{:S(2)}) collective-permute-start(bf16[32,3200]{1,0:T(8,128)(2,1)S(1)} %collective-permute-done.1.refs_4_), channel_id=1, source_target_pairs={{0,1},{1,0},{2,3},{3,2},{4,5},{5,4},{6,7},{7,6},{8,9},{9,8},{10,11... | collective-permute-start | bytes 614408 | tf_op jit(solution)/shard_map/vision_gather/ppermute | solution.py:38
  47.3 16.7 %collective-permute-start.6 = (bf16[16,3200]{1,0:T(8,128)(2,1)S(1)}, bf16[16,3200]{1,0:T(8,128)(2,1)}, u32[]{:S(2)}, u32[]{:S(2)}) collective-permute-start(bf16[16,3200]{1,0:T(8,128)(2,1)S(1)} %collective-permute-done.2.refs_2_), channel_id=1, source_target_pairs={{0,1},{1,0},{2,3},{3,2},{4,5},{5,4},{6,7},{7,6},{8,9},{9,8},{10,11... | collective-permute-start | bytes 307208 | tf_op jit(solution)/shard_map/vision_gather/ppermute | solution.py:38
  49.6 16.0 %collective-permute-start.18 = (bf16[512,128]{1,0:T(8,128)(2,1)S(1)}, bf16[512,128]{1,0:T(8,128)(2,1)}, u32[]{:S(2)}, u32[]{:S(2)}) collective-permute-start(bf16[512,128]{1,0:T(8,128)(2,1)S(1)} %bitcast.14), channel_id=1, source_target_pairs={{0,6},{1,7},{2,0},{3,1},{4,2},{5,3},{6,4},{7,5},{8,14},{9,15},{10,... | collective-permute-start | bytes 393224 | tf_op jit(solution)/shard_map/image_grad_gather/ppermute | solution.py:30
  52.7 13.3 %collective-permute-start.19 = (bf16[512,128]{1,0:T(8,128)(2,1)S(1)}, bf16[512,128]{1,0:T(8,128)(2,1)}, u32[]{:S(2)}, u32[]{:S(2)}) collective-permute-start(bf16[512,128]{1,0:T(8,128)(2,1)S(1)} %bitcast.15), channel_id=1, source_target_pairs={{0,4},{1,5},{2,6},{3,7},{4,0},{5,1},{6,2},{7,3},{8,12},{9,13},{10,... | collective-permute-start | bytes 393224 | tf_op jit(solution)/shard_map/image_grad_gather/ppermute | solution.py:34
  53.3 12.8 %collective-permute-start.20 = (bf16[512,128]{1,0:T(8,128)(2,1)S(1)}, bf16[512,128]{1,0:T(8,128)(2,1)}, u32[]{:S(2)}, u32[]{:S(2)}) collective-permute-start(bf16[512,128]{1,0:T(8,128)(2,1)S(1)} %bitcast.16), channel_id=1, source_target_pairs={{0,2},{1,3},{2,4},{3,5},{4,6},{5,7},{6,0},{7,1},{8,10},{9,11},{10,... | collective-permute-start | bytes 393224 | tf_op jit(solution)/shard_map/image_grad_gather/ppermute | solution.py:26
  65.4 17.2 %collective-permute-start.21 = (bf16[512,128]{1,0:T(8,128)(2,1)S(1)}, bf16[512,128]{1,0:T(8,128)(2,1)S(1)}, u32[]{:S(2)}, u32[]{:S(2)}) collective-permute-start(bf16[512,128]{1,0:T(8,128)(2,1)S(1)} %bitcast.17), channel_id=1, source_target_pairs={{0,1},{1,0},{2,3},{3,2},{4,5},{5,4},{6,7},{7,6},{8,9},{9,8},{10,11... | collective-permute-start | bytes 393224 | tf_op jit(solution)/shard_map/image_grad_gather/ppermute | solution.py:38
  65.6 17.3 %collective-permute-start.22 = (bf16[512,128]{1,0:T(8,128)(2,1)}, bf16[512,128]{1,0:T(8,128)(2,1)S(1)}, u32[]{:S(2)}, u32[]{:S(2)}) collective-permute-start(bf16[512,128]{1,0:T(8,128)(2,1)} %collective-permute-done.18.refs_1_), channel_id=1, source_target_pairs={{0,1},{1,0},{2,3},{3,2},{4,5},{5,4},{6,7},{7,6},{8,9},{9,8},{10,11... | collective-permute-start | bytes 393224 | tf_op jit(solution)/shard_map/image_grad_gather/ppermute | solution.py:38
  66.0 17.0 %collective-permute-start.23 = (bf16[512,128]{1,0:T(8,128)(2,1)}, bf16[512,128]{1,0:T(8,128)(2,1)S(1)}, u32[]{:S(2)}, u32[]{:S(2)}) collective-permute-start(bf16[512,128]{1,0:T(8,128)(2,1)} %collective-permute-done.19.refs_2_), channel_id=1, source_target_pairs={{0,1},{1,0},{2,3},{3,2},{4,5},{5,4},{6,7},{7,6},{8,9},{9,8},{10,11... | collective-permute-start | bytes 393224 | tf_op jit(solution)/shard_map/image_grad_gather/ppermute | solution.py:38
  66.1 16.8 %collective-permute-start.24 = (bf16[512,128]{1,0:T(8,128)(2,1)}, bf16[512,128]{1,0:T(8,128)(2,1)S(1)}, u32[]{:S(2)}, u32[]{:S(2)}) collective-permute-start(bf16[512,128]{1,0:T(8,128)(2,1)} %collective-permute-done.20.refs_3_), channel_id=1, source_target_pairs={{0,1},{1,0},{2,3},{3,2},{4,5},{5,4},{6,7},{7,6},{8,9},{9,8},{10,11... | collective-permute-start | bytes 393224 | tf_op jit(solution)/shard_map/image_grad_gather/ppermute | solution.py:38
  82.4 19.9 %collective-permute-start.9 = (f32[6,128]{1,0:T(8,128)}, f32[6,128]{1,0:T(8,128)}, u32[]{:S(2)}, u32[]{:S(2)}) collective-permute-start(f32[6,128]{1,0:T(8,128)} %pad_maximum_fusion), channel_id=1, source_target_pairs={{0,1},{1,0},{2,3},{3,2},{4,5},{5,4},{6,7},{7,6},{8,9},{9,8},{10,11... | collective-permute-start | bytes 9224 | tf_op jit(solution)/shard_map/squares_sum/ppermute | solution.py:38
  82.7 39.3 %collective-permute-start.13 = (bf16[4,256,256]{2,1,0:T(8,128)(2,1)}, bf16[4,256,256]{2,1,0:T(8,128)(2,1)S(1)}, u32[]{:S(2)}, u32[]{:S(2)}) collective-permute-start(bf16[4,256,256]{2,1,0:T(8,128)(2,1)} %get-tuple-element.37), channel_id=1, source_target_pairs={{0,1},{1,0},{2,3},{3,2},{4,5},{5,4},{6,7},{7,6},{8,9},{9,8},{10,11... | collective-permute-start | bytes 1572872 | tf_op jit(solution)/shard_map/image_key_value_sum/ppermute | solution.py:38
  122.0 21.8 %collective-permute-start.29 = (bf16[128,3200]{1,0:T(8,128)(2,1)}, bf16[128,3200]{1,0:T(8,128)(2,1)S(1)}, u32[]{:S(2)}, u32[]{:S(2)}) collective-permute-start(bf16[128,3200]{1,0:T(8,128)(2,1)} %get-tuple-element.53), channel_id=1, source_target_pairs={{0,1},{1,0},{2,3},{3,2},{4,5},{5,4},{6,7},{7,6},{8,9},{9,8},{10,11... | collective-permute-start | bytes 2457608 | tf_op jit(solution)/shard_map/d_vis_sum/ppermute | solution.py:38
  136.0 16.9 %all-to-all-start = ((bf16[32,16,128]{2,1,0:T(8,128)(2,1)}), bf16[32,16,128]{2,1,0:T(8,128)(2,1)S(1)}, u32[]{:S(2)}, u32[]{:S(2)}) async-start(bf16[32,16,128]{2,1,0:T(8,128)(2,1)} %bitcast.2), calls=%async_computation.1 | async-start | bytes 262144 | tf_op jit(solution)/shard_map/image_out_spread/all_to_all | solution.py:482
  149.4 15.3 %collective-permute-start.30 = (bf16[32,3200]{1,0:T(8,128)(2,1)}, bf16[32,3200]{1,0:T(8,128)(2,1)}, u32[]{:S(2)}, u32[]{:S(2)}) collective-permute-start(bf16[32,3200]{1,0:T(8,128)(2,1)} %get-tuple-element.55), channel_id=1, source_target_pairs={{0,2},{1,3},{2,4},{3,5},{4,6},{5,7},{6,0},{7,1},{8,10},{9,11},{10,... | collective-permute-start | bytes 614408 | tf_op jit(solution)/shard_map/d_vis_sum/ppermute | solution.py:26
  154.2 22.7 %all-to-all-start.1 = ((bf16[32,2,16,128]{3,2,1,0:T(8,128)(2,1)}), bf16[32,2,16,128]{3,2,1,0:T(8,128)(2,1)S(1)}, u32[]{:S(2)}, u32[]{:S(2)}) async-start(bf16[32,2,16,128]{3,2,1,0:T(8,128)(2,1)} %bitcast.11), calls=%async_computation.2 | async-start | bytes 524288 | tf_op jit(solution)/shard_map/image_out_collect/all_to_all | solution.py:485
  166.4 12.9 %collective-permute-start.32 = (bf16[16,3200]{1,0:T(8,128)(2,1)}, bf16[16,3200]{1,0:T(8,128)(2,1)S(1)}, u32[]{:S(2)}, u32[]{:S(2)}) collective-permute-start(bf16[16,3200]{1,0:T(8,128)(2,1)} %add_convert_fusion.1), channel_id=1, source_target_pairs={{0,2},{1,3},{2,4},{3,5},{4,6},{5,7},{6,0},{7,1},{8,10},{9,11},{10,... | collective-permute-start | bytes 307208 | tf_op jit(solution)/shard_map/d_vis_sum/ppermute | solution.py:26
  (77 other events, 522.7 us)
Sparse Core Ops, SparseCore 0:
  10.2 33.3 all-gather.1
  64.1 34.2 reduce-scatter.1
